TPU v7x, 128 devices: a whole 4x4x4 slice. The times are simulated.
128 devices in a mesh: section: 4 (over x_hi, core), tile: 32 (over x_lo, z, y).
Axes of the slice: x: 4 (x_hi: 2, x_lo: 2; x = x_hi * 2 + x_lo), y: 4, z: 4, core: 2. Of those that a mesh axis runs over, the one named last changes fastest.
Arguments:
- layer_input: bfloat16 [4, 3, 32, 16, 32, 128], P('section', None, 'tile'), may hold values from -6 to 6
- hidden_prev: bfloat16 [4, 3, 32, 16, 32, 128], P('section', None, 'tile'), may hold values from -0.8984375 to 0.8984375
- cell_prev: float32 [4, 3, 32, 16, 32, 128], P('section', None, 'tile'), may hold values from -6 to 6
- out_cot: bfloat16 [3, 32, 16, 32, 128], P(None, 'tile'), may hold values from -18 to 18
- bias: float32 [4, 512], P('section'), may hold values from -1 to 2
- master: float32 [4, 2304, 512], P('section', 'tile'), may hold values from -0.375 to 0.375
- moment1: float32 [4, 2304, 512], P('section', 'tile'), may hold values from -6 to 6
- moment2: float32 [4, 2304, 512], P('section', 'tile'), may hold values from 1 to 100
Outputs:
- input_cot: bfloat16 [4, 3, 32, 16, 32, 128], P('section', None, 'tile')
- new_master: float32 [4, 2304, 512], P('section', 'tile')
- new_moment1: float32 [4, 2304, 512], P('section', 'tile')
- new_moment2: float32 [4, 2304, 512], P('section', 'tile')
All inputs are finite; a program needn't handle non-finite values.
Results may differ from a plain program's by a relative error of at most 0.012.
Values may be sent and summed in bfloat16 or wider, within the bound.
No kernel may reach another device: no remote copies, remote signals or barrier semaphores. Data moves between devices by JAX's collectives and lax.ppermute only.
A program may use at most 128 MiB of HBM per device.

v0:
```python
import functools

import jax
import jax.numpy as jnp
from jax import lax
from jax.experimental import pallas as pl
from jax.experimental.pallas import tpu as pltpu
from jax.sharding import PartitionSpec as P

TILE_ROWS = 4
BF = jnp.bfloat16
F32 = jnp.float32
SIDE = 8
LEAD = 16
VMEM_LIMIT = 56 * 1024 * 1024


def chunks(size, most):
    units = size // 16
    count = -(-units * 16 // most)
    out, at = [], 0
    for i in range(count):
        end = units * (i + 1) // count
        out.append((at * 16, (end - at) * 16))
        at = end
    return out


def in_vmem(shape, dtype):
    return pltpu.VMEM(shape, dtype)


def sigmoid(x):
    return 0.5 * jnp.tanh(0.5 * x) + 0.5


def gates_kernel(pitch, cells, width, zs_ref, ext_ref, mask_ref, kernel_ref, bias_ref, fac_ref):
    depth = 6 * width
    for start, size in chunks(cells, 480):
        total = bias_ref[...]
        for a in range(3):
            total = total + jnp.dot(
                zs_ref[pl.ds(start + a * pitch, size), :],
                kernel_ref[a * depth : (a + 1) * depth, :],
                preferred_element_type=F32,
            )
        here = pl.ds(start, size)
        mask = mask_ref[here, :].astype(F32)
        c_prev = ext_ref[pl.ds(start + pitch, size), 2 * width : 3 * width].astype(F32)
        i = sigmoid(total[:, :width])
        f = sigmoid(total[:, width : 2 * width])
        g = jnp.tanh(total[:, 2 * width : 3 * width])
        o = sigmoid(total[:, 3 * width :])
        tc = jnp.tanh(f * c_prev + i * g)
        fac_ref[here, 0:width] = o * (1.0 - tc * tc)
        fac_ref[here, width : 2 * width] = mask * g * i * (1.0 - i)
        fac_ref[here, 2 * width : 3 * width] = mask * c_prev * f * (1.0 - f)
        fac_ref[here, 3 * width : 4 * width] = mask * i * (1.0 - g * g)
        fac_ref[here, 4 * width : 5 * width] = mask * tc * o * (1.0 - o)
        fac_ref[here, 5 * width : 6 * width] = f


def step_kernel(step, layers, frames, pitch, rows, cols, width, *refs):
    ids_ref, kernel_t_ref = refs[0], refs[1]
    picks = [f for f in range(frames) if 0 <= frames - 1 - step + layers - 1 - f <= layers - 1]
    fac_refs = refs[2 : 2 + len(picks)]
    at = 2 + len(picks)
    first, tops = step == 0, step < frames
    ext_ref = refs[at] if tops else None
    at += 1 if tops else 0
    if not first:
        inc_ref, dh_ref, dc_ref = refs[at : at + 3]
        at += 3
    dx_ref, dxi_ref, dgi_ref, dhn_ref, dcn_ref, d_ref, p_ref = refs[at:]
    margin = frames + layers - 1 - step
    size_d = LEAD + (rows + 2 * margin) * pitch
    size_z = LEAD + (rows + 2 * margin - 2) * pitch
    frame = ids_ref[0] - step
    ngate = 4 * width

    def point(fac_ref, top_frame, pick):
        start_frame = pick == frames - 1
        for start, size in chunks(size_d, 256):
            here = pl.ds(start, size)
            there = pl.ds(start + step * pitch, size)
            if tops and pick == top_frame:
                own = ext_ref[pl.ds(start + (step + 1) * pitch, size), 3 * width :]
                above = own.astype(F32)
            else:
                above = inc_ref[here, :].astype(F32)
            dh = above
            if not start_frame:
                dh = dh + dh_ref[here, :]
            dc = dh * fac_ref[there, 0:width]
            if not start_frame:
                dc = dc + dc_ref[here, :]
            d_ref[here, 0:width] = (dc * fac_ref[there, width : 2 * width]).astype(BF)
            d_ref[here, width : 2 * width] = (dc * fac_ref[there, 2 * width : 3 * width]).astype(BF)
            d_ref[here, 2 * width : 3 * width] = (dc * fac_ref[there, 3 * width : 4 * width]).astype(BF)
            d_ref[here, 3 * width :] = (dh * fac_ref[there, 4 * width : 5 * width]).astype(BF)
            lo, hi = max(start, pitch), min(start + size, pitch + size_z)
            if hi > lo:
                rec = dc * fac_ref[there, 5 * width :]
                dcn_ref[lo - pitch : hi - pitch, :] = rec[lo - start : hi - start, :]

    top_frame = frames - 1 - step
    for number, pick in enumerate(picks):
        pl.when(frame == pick)(functools.partial(point, fac_refs[number], top_frame, pick))

    @pl.when((frame >= 0) & (frame < frames))
    def _():
        for row in range(rows):
            dgi_ref[row * cols : (row + 1) * cols, :] = d_ref[
                pl.ds(LEAD + (row + margin) * pitch, cols), :
            ]
        for side in range(3):
            p_ref[0:8, side * 2 * width : (side + 1) * 2 * width] = jnp.zeros((8, 2 * width), F32)
            p_ref[8 + size_z : 16 + size_z, side * 2 * width : (side + 1) * 2 * width] = jnp.zeros(
                (8, 2 * width), F32
            )
        for start, size in chunks(size_z, 448):
            total = None
            for a in range(3):
                part = jnp.dot(
                    d_ref[pl.ds(start + (2 - a) * pitch, size), :],
                    kernel_t_ref[a * ngate : (a + 1) * ngate, :],
                    preferred_element_type=F32,
                )
                total = part if total is None else total + part
            p_ref[pl.ds(8 + start, size), :] = total
        for start, size in chunks(size_z, 256):
            dz = (
                p_ref[pl.ds(8 + start, size), 2 * width : 4 * width]
                + p_ref[pl.ds(9 + start, size), 0 : 2 * width]
                + p_ref[pl.ds(7 + start, size), 4 * width :]
            )
            dx_ref[pl.ds(start, size), :] = dz[:, :width].astype(BF)
            dhn_ref[pl.ds(start, size), :] = dz[:, width:]
        for row in range(rows):
            dxi_ref[row * cols : (row + 1) * cols, :] = dx_ref[
                pl.ds(LEAD + (row + margin - 1) * pitch, cols), :
            ]


def spec_v():
    return pl.BlockSpec(memory_space=pltpu.VMEM)


def spec_s():
    return pl.BlockSpec(memory_space=pltpu.SMEM)


def row_pairs(ntile, ncols, by):
    return [(i, i + by * ncols) for i in range(ntile) if 0 <= i + by * ncols < ntile]


def col_pairs(ntile, ncols, by):
    return [(i, i + by) for i in range(ntile) if 0 <= i % ncols + by < ncols]


def on_device(layer_input, hidden_prev, cell_prev, out_cot, bias, master, moment1, moment2):
    frames, rows, cols, width = (layer_input.shape[i] for i in (1, 3, 4, 5))
    ngate = 4 * width
    layers = lax.axis_size("section")
    layer = lax.axis_index("section")
    ntile = lax.axis_size("tile")
    tile = lax.axis_index("tile")
    ncols = ntile // TILE_ROWS
    pitch = cols + 2 * SIDE
    edge = frames + layers - 1

    own_rows = master[0].astype(BF)
    kernel = lax.all_to_all(jnp.tile(own_rows, (ntile, 1)), "tile", 0, 0, tiled=True)
    kernel_t = kernel.reshape(3, 6 * width, ngate).transpose(0, 2, 1).reshape(3 * ngate, 6 * width)

    packed = jnp.concatenate(
        [layer_input[0, :, 0], hidden_prev[0, :, 0], cell_prev[0, :, 0].astype(BF), out_cot[:, 0]], -1
    )
    ext = [None] * frames
    for f in reversed(range(frames)):
        deep = edge + 1 - (frames - 1 - f)
        block = packed[f]
        above = lax.ppermute(block[rows - deep :], "tile", row_pairs(ntile, ncols, 1))
        below = lax.ppermute(block[:deep], "tile", row_pairs(ntile, ncols, -1))
        tall = jnp.concatenate([above, block, below], 0)
        left = lax.ppermute(tall[:, cols - SIDE :], "tile", col_pairs(ntile, ncols, 1))
        right = lax.ppermute(tall[:, :SIDE], "tile", col_pairs(ntile, ncols, -1))
        wide = jnp.concatenate([left, tall, right], 1)
        gap = edge + 1 - deep
        flat = wide.reshape(-1, 4 * width)
        ext[f] = jnp.pad(
            flat, ((LEAD - SIDE + gap * pitch, SIDE + gap * pitch), (0, 0))
        )
    size_e = LEAD + (rows + 2 * edge + 2) * pitch
    size_d = LEAD + (rows + 2 * edge) * pitch

    at = jnp.arange(size_d, dtype=jnp.int32) - LEAD + SIDE
    row_at = at // pitch - edge + (tile // ncols) * rows
    col_at = at % pitch - SIDE + (tile % ncols) * cols
    inside = (row_at >= 0) & (row_at < TILE_ROWS * rows) & (col_at >= 0) & (col_at < ncols * cols)
    mask = jnp.broadcast_to(inside[:, None], (size_d, width)).astype(BF)

    params = pltpu.CompilerParams(vmem_limit_bytes=VMEM_LIMIT)
    facs, patches = [None] * frames, [None] * frames
    for f in reversed(range(frames)):
        z = ext[f][:, : 2 * width]
        none = jnp.zeros((1, 2 * width), BF)
        zs = jnp.concatenate(
            [jnp.concatenate([none, z[:-1]], 0), z, jnp.concatenate([z[1:], none], 0)], -1
        )
        inner = zs[LEAD:].reshape(rows + 2 * edge + 2, pitch, 6 * width)[edge : edge + rows + 2, :cols]
        patches[f] = jnp.concatenate(
            [inner[a : a + rows].reshape(rows * cols, 6 * width) for a in range(3)], -1
        )
        facs[f] = pl.pallas_call(
            functools.partial(gates_kernel, pitch, size_d, width),
            out_shape=in_vmem((size_d, 6 * width), F32),
            in_specs=[spec_v()] * 5,
            out_specs=spec_v(),
            compiler_params=params,
            cost_estimate=pl.CostEstimate(
                flops=2 * size_d * 18 * width * ngate, bytes_accessed=10 << 20, transcendentals=size_d * 5 * width
            ),
        )(zs, ext[f], mask, kernel, bias)

    ids = (frames - 1 + layers - 1 - layer).astype(jnp.int32).reshape(1)
    state = []
    sent_dx, kept = [], []
    steps = layers + frames - 1
    for step in range(steps):
        margin = edge - step
        size_z = LEAD + (rows + 2 * margin - 2) * pitch
        picks = [f for f in range(frames) if 0 <= frames - 1 - step + layers - 1 - f <= layers - 1]
        args = [ids, kernel_t] + [facs[f] for f in picks]
        if step < frames:
            args.append(ext[frames - 1 - step])
        args += state
        dx, dxi, dgi, dh_rec, dc_rec = pl.pallas_call(
            functools.partial(step_kernel, step, layers, frames, pitch, rows, cols, width),
            out_shape=(
                jax.ShapeDtypeStruct((size_z, width), BF),
                jax.ShapeDtypeStruct((rows * cols, width), BF),
                jax.ShapeDtypeStruct((rows * cols, ngate), BF),
                in_vmem((size_z, width), F32),
                in_vmem((size_z, width), F32),
            ),
            in_specs=[spec_s()] + [spec_v()] * (len(args) - 1),
            out_specs=(spec_v(),) * 5,
            scratch_shapes=[
                pltpu.VMEM((size_z + 2 * pitch, ngate), BF),
                pltpu.VMEM((size_z + 16, 6 * width), F32),
            ],
            compiler_params=params,
            cost_estimate=pl.CostEstimate(
                flops=2 * size_z * 18 * width * ngate, bytes_accessed=10 << 20, transcendentals=0
            ),
        )(*args)
        sent_dx.append(dxi)
        kept.append(dgi)
        if step < steps - 1:
            pairs = [
                (i, i - 1)
                for i in range(1, layers)
                if 0 <= frames - 1 - step + layers - 1 - i < frames
            ]
            state = [lax.ppermute(dx, "section", pairs), dh_rec, dc_rec]

    first = layers - 1 - layer
    late = lax.dynamic_slice_in_dim(jnp.stack(kept), first, frames, 0)
    flat_dgates = late.reshape(frames * rows * cols, ngate)
    all_patches = jnp.concatenate([patches[f] for f in reversed(range(frames))], 0)
    partial = lax.dot_general(
        all_patches, flat_dgates, (((0,), (0,)), ((), ())), preferred_element_type=F32
    ).astype(BF)
    arrived = lax.all_to_all(partial, "tile", 0, 0, tiled=True)
    cots = lax.dynamic_slice_in_dim(jnp.stack(sent_dx), first, frames, 0)
    input_cot = jnp.flip(cots, 0).reshape(frames, rows, cols, width)
    grad_rows = jnp.sum(arrived.reshape(ntile, -1, ngate).astype(F32), 0)
    new_moment1 = 0.9 * moment1[0] + 0.1 * grad_rows
    new_moment2 = 0.999 * moment2[0] + 0.001 * grad_rows * grad_rows
    fix1 = 1.0 - 0.9**10
    fix2 = 1.0 - 0.999**10
    step_size = new_moment1 / fix1 / (jnp.sqrt(new_moment2 / fix2) + 1e-08)
    new_master = master[0] - 0.001 * step_size - 0.0001 * master[0]
    return (input_cot[None, :, None], new_master[None], new_moment1[None], new_moment2[None])


def solution(mesh):
    return jax.shard_map(
        on_device,
        mesh=mesh,
        in_specs=(
            P("section", None, "tile", None, None, None),
            P("section", None, "tile", None, None, None),
            P("section", None, "tile", None, None, None),
            P(None, "tile", None, None, None),
            P("section", None),
            P("section", "tile", None),
            P("section", "tile", None),
            P("section", "tile", None),
        ),
        out_specs=(
            P("section", None, "tile", None, None, None),
            P("section", "tile", None),
            P("section", "tile", None),
            P("section", "tile", None),
        ),
        check_vma=False,
    )
```

profile of v0, /device:TPU:0, one launch (start us, length us, event | category | flops | bytes accessed | tf_op | source)
XLA Modules:
  0.0 303.7 jit_solution(10120295217199354609)
XLA Ops:
  1.6 1.6 tile.2
  3.2 9.5 %all-to-all-start = ((bf16[32,72,512]{2,1,0:T(8,128)(2,1)}), bf16[32,72,512]{2,1,0:T(8,128)(2,1)S(1)}, u32[]{:S(2)}, u32[]{:S(2)}) async-start(bf16[32,72,512]{2,1,0:T(8,128)(2,1)} %tile.2), calls=%async_computation | async-start | bytes 4718592 | tf_op jit(solution)/shard_map/all_to_all | solution.py:173
  12.7 1.2 fusion.33
  14.9 1.3 collective-permute-start.1
  17.0 1.3 collective-permute-start.10
  18.3 7.3 %collective-permute-start.9 = (bf16[5,32,512]{2,1,0:T(8,128)(2,1)}, bf16[5,32,512]{2,1,0:T(8,128)(2,1)}, u32[]{:S(2)}, u32[]{:S(2)}) collective-permute-start(bf16[5,32,512]{2,1,0:T(8,128)(2,1)} %get-tuple-element.78), channel_id=1, source_target_pairs={{0,8},{1,9},{2,10},{3,11},{4,12},{5,13},{6,14},{7,15},{8,16},{9,17... | collective-permute-start | bytes 491528 | tf_op jit(solution)/shard_map/ppermute | solution.py:183
  26.4 1.3 collective-permute-start.5
  27.7 7.0 %collective-permute-start.4 = (bf16[6,32,512]{2,1,0:T(8,128)(2,1)}, bf16[6,32,512]{2,1,0:T(8,128)(2,1)}, u32[]{:S(2)}, u32[]{:S(2)}) collective-permute-start(bf16[6,32,512]{2,1,0:T(8,128)(2,1)} %get-tuple-element.83), channel_id=1, source_target_pairs={{0,8},{1,9},{2,10},{3,11},{4,12},{5,13},{6,14},{7,15},{8,16},{9,17... | collective-permute-start | bytes 589832 | tf_op jit(solution)/shard_map/ppermute | solution.py:183
  35.6 15.8 %collective-permute-done.10 = bf16[5,32,512]{2,1,0:T(8,128)(2,1)} collective-permute-done((bf16[5,32,512]{2,1,0:T(8,128)(2,1)}, bf16[5,32,512]{2,1,0:T(8,128)(2,1)}, u32[]{:S(2)}, u32[]{:S(2)}) %collective-permute-start.10) | collective-permute-done | bytes 163872 | tf_op jit(solution)/shard_map/ppermute | solution.py:184
  51.5 5.5 %collective-permute-start = (bf16[7,32,512]{2,1,0:T(8,128)(2,1)}, bf16[7,32,512]{2,1,0:T(8,128)(2,1)S(1)}, u32[]{:S(2)}, u32[]{:S(2)}) collective-permute-start(bf16[7,32,512]{2,1,0:T(8,128)(2,1)} %get-tuple-element.85), channel_id=1, source_target_pairs={{0,8},{1,9},{2,10},{3,11},{4,12},{5,13},{6,14},{7,15},{8,16},{9,17... | collective-permute-start | bytes 688136 | tf_op jit(solution)/shard_map/ppermute | solution.py:183
  57.9 1.3 collective-permute-start.12
  59.2 4.6 %collective-permute-start.11 = (bf16[26,8,512]{2,1,0:T(8,128)(2,1)S(1)}, bf16[26,8,512]{2,1,0:T(8,128)(2,1)S(1)}, u32[]{:S(2)}, u32[]{:S(2)}) collective-permute-start(bf16[26,8,512]{2,1,0:T(8,128)(2,1)S(1)} %get-tuple-element.97), channel_id=1, source_target_pairs={{0,1},{1,2},{2,3},{3,4},{4,5},{5,6},{6,7},{8,9},{9,10},{10,11},{11... | collective-permute-start | bytes 638984 | tf_op jit(solution)/shard_map/ppermute | solution.py:186
  64.8 1.3 collective-permute-start.7
  66.1 4.6 %collective-permute-start.6 = (bf16[28,8,512]{2,1,0:T(8,128)(2,1)S(1)}, bf16[28,8,512]{2,1,0:T(8,128)(2,1)S(1)}, u32[]{:S(2)}, u32[]{:S(2)}) collective-permute-start(bf16[28,8,512]{2,1,0:T(8,128)(2,1)S(1)} %get-tuple-element.95), channel_id=1, source_target_pairs={{0,1},{1,2},{2,3},{3,4},{4,5},{5,6},{6,7},{8,9},{9,10},{10,11},{11... | collective-permute-start | bytes 688136 | tf_op jit(solution)/shard_map/ppermute | solution.py:186
  71.6 1.3 collective-permute-start.3
  72.9 4.7 %collective-permute-start.2 = (bf16[30,8,512]{2,1,0:T(8,128)(2,1)S(1)}, bf16[30,8,512]{2,1,0:T(8,128)(2,1)S(1)}, u32[]{:S(2)}, u32[]{:S(2)}) collective-permute-start(bf16[30,8,512]{2,1,0:T(8,128)(2,1)S(1)} %get-tuple-element.93), channel_id=1, source_target_pairs={{0,1},{1,2},{2,3},{3,4},{4,5},{5,6},{6,7},{8,9},{9,10},{10,11},{11... | collective-permute-start | bytes 737288 | tf_op jit(solution)/shard_map/ppermute | solution.py:186
  77.6 1.1 pad_maximum_fusion.3
  78.8 1.2 pad.20.ext_ref.refs_5_
  80.0 1.2 pad_maximum_fusion.2
  81.7 1.2 pad.19.ext_ref.refs_4_
  84.8 1.8 fusion.55
  86.7 1.5 fusion.54
  89.3 1.2 pad.18.ext_ref.refs_3_
  91.3 1.2 copy-done.16
  92.5 1.5 fusion.53
  94.0 2.9 copy.14
  97.8 6.8 %shard_map.111.refs_2_.refs_3_.refs_4_ = f32[1360,768]{1,0:T(8,128)S(1)} custom-call(bf16[1456,768]{1,0:T(8,128)(2,1)} %copy-done.16, bf16[1456,512]{1,0:T(8,128)(2,1)} %pad.18.ext_ref.refs_3_, bf16[1360,128]{1,0:T(8,128)(2,1)} %broadcast_in_dim.2.mask_ref, bf16[2304,512]{1,0:T(8,128)(2,1)} %bitcast.106, f32[1,512]{1,0:T(1,128)} %bias_ref.5), custom_call_target="tpu_custom_call" | custom-call | flops 3208642560 | bytes 10485760 | tf_op jit(solution)/shard_map/pallas_call | solution.py:215
  104.7 1.9 copy-done.2
  106.6 4.3 %shard_map.112 = (bf16[1264,128]{1,0:T(8,128)(2,1)}, bf16[512,128]{1,0:T(8,128)(2,1)}, bf16[512,512]{1,0:T(8,128)(2,1)}, f32[1264,128]{1,0:T(8,128)S(1)}, f32[1264,128]{1,0:T(8,128)S(1)}) custom-call(s32[1]{0:T(128)} %bitcast.refs_0_, bf16[1536,768]{1,0:T(8,128)(2,1)} %bitcast.87, f32[1360,768]{1,0:T(8,128)} %copy-done.2, bf16[1456,512]{1,0:T(8,128)(2,1)} %pad.18.ext_ref.refs_3_), custom_call_target="tpu_custom_call" | custom-call | flops 2982150144 | bytes 10485760 | tf_op jit(solution)/shard_map/pallas_call | solution.py:238
  114.6 6.7 %shard_map.113.refs_2_.refs_3_ = f32[1360,768]{1,0:T(8,128)S(1)} custom-call(bf16[1456,768]{1,0:T(8,128)(2,1)} %copy-done.15, bf16[1456,512]{1,0:T(8,128)(2,1)} %pad.19.ext_ref.refs_4_, bf16[1360,128]{1,0:T(8,128)(2,1)} %broadcast_in_dim.2.mask_ref, bf16[2304,512]{1,0:T(8,128)(2,1)} %bitcast.107, f32[1,512]{1,0:T(1,128)} %bias_ref.5), custom_call_target="tpu_custom_call" | custom-call | flops 3208642560 | bytes 10485760 | tf_op jit(solution)/shard_map/pallas_call | solution.py:215
  121.3 1.9 copy-done.1
  123.9 5.9 %shard_map.114 = (bf16[1168,128]{1,0:T(8,128)(2,1)}, bf16[512,128]{1,0:T(8,128)(2,1)}, bf16[512,512]{1,0:T(8,128)(2,1)}, f32[1168,128]{1,0:T(8,128)S(1)}, f32[1168,128]{1,0:T(8,128)S(1)}) custom-call(s32[1]{0:T(128)} %bitcast.refs_0_, bf16[1536,768]{1,0:T(8,128)(2,1)} %bitcast.88, f32[1360,768]{1,0:T(8,128)} %copy-done.1, f32[1360,768]{1,0:T(8,128)} %copy-done.2, ...), custom_call_target="tpu_custom_call" | custom-call | flops 2755657728 | bytes 10485760 | tf_op jit(solution)/shard_map/pallas_call | solution.py:238
  132.2 6.7 %shard_map.115.refs_2_ = f32[1360,768]{1,0:T(8,128)S(1)} custom-call(bf16[1456,768]{1,0:T(8,128)(2,1)} %copy-done.14, bf16[1456,512]{1,0:T(8,128)(2,1)} %pad.20.ext_ref.refs_5_, bf16[1360,128]{1,0:T(8,128)(2,1)} %broadcast_in_dim.2.mask_ref, bf16[2304,512]{1,0:T(8,128)(2,1)} %bitcast.108, f32[1,512]{1,0:T(1,128)} %bias_ref.5), custom_call_target="tpu_custom_call" | custom-call | flops 3208642560 | bytes 10485760 | tf_op jit(solution)/shard_map/pallas_call | solution.py:215
  138.9 1.9 copy-done
  141.5 7.1 %shard_map.116 = (bf16[1072,128]{1,0:T(8,128)(2,1)}, bf16[512,128]{1,0:T(8,128)(2,1)}, bf16[512,512]{1,0:T(8,128)(2,1)}, f32[1072,128]{1,0:T(8,128)S(1)}, f32[1072,128]{1,0:T(8,128)S(1)}) custom-call(s32[1]{0:T(128)} %bitcast.refs_0_, bf16[1536,768]{1,0:T(8,128)(2,1)} %bitcast.89, f32[1360,768]{1,0:T(8,128)} %copy-done, f32[1360,768]{1,0:T(8,128)} %copy-done.1, ...), custom_call_target="tpu_custom_call" | custom-call | flops 2529165312 | bytes 10485760 | tf_op jit(solution)/shard_map/pallas_call | solution.py:238
  150.2 1.3 collective-permute-start.14
  152.6 7.8 %collective-permute-done.14.refs_5_ = bf16[1072,128]{1,0:T(8,128)(2,1)S(1)} collective-permute-done((bf16[1072,128]{1,0:T(8,128)(2,1)}, bf16[1072,128]{1,0:T(8,128)(2,1)S(1)}, u32[]{:S(2)}, u32[]{:S(2)}) %collective-permute-start.14) | collective-permute-done | bytes 274464 | tf_op jit(solution)/shard_map/ppermute | solution.py:266
  161.2 21.9 %shard_map.117 = (bf16[976,128]{1,0:T(8,128)(2,1)}, bf16[512,128]{1,0:T(8,128)(2,1)}, bf16[512,512]{1,0:T(8,128)(2,1)}, f32[976,128]{1,0:T(8,128)S(1)}, f32[976,128]{1,0:T(8,128)S(1)}) custom-call(s32[1]{0:T(128)} %bitcast.refs_0_, bf16[1536,768]{1,0:T(8,128)(2,1)} %bitcast.90, f32[1360,768]{1,0:T(8,128)} %copy-done, f32[1360,768]{1,0:T(8,128)} %copy-done.1, ...), custom_call_target="tpu_custom_call" | custom-call | flops 2302672896 | bytes 10485760 | tf_op jit(solution)/shard_map/pallas_call | solution.py:238
  184.6 1.3 collective-permute-start.15
  187.0 8.3 %collective-permute-done.15.refs_4_ = bf16[976,128]{1,0:T(8,128)(2,1)S(1)} collective-permute-done((bf16[976,128]{1,0:T(8,128)(2,1)}, bf16[976,128]{1,0:T(8,128)(2,1)S(1)}, u32[]{:S(2)}, u32[]{:S(2)}) %collective-permute-start.15) | collective-permute-done | bytes 249888 | tf_op jit(solution)/shard_map/ppermute | solution.py:266
  196.0 7.9 %shard_map.118 = (bf16[880,128]{1,0:T(8,128)(2,1)}, bf16[512,128]{1,0:T(8,128)(2,1)}, bf16[512,512]{1,0:T(8,128)(2,1)}, f32[880,128]{1,0:T(8,128)S(1)}, f32[880,128]{1,0:T(8,128)S(1)}) custom-call(s32[1]{0:T(128)} %bitcast.refs_0_, bf16[1536,768]{1,0:T(8,128)(2,1)} %bitcast.91, f32[1360,768]{1,0:T(8,128)} %copy-done, f32[1360,768]{1,0:T(8,128)} %copy-done.1, ...), custom_call_target="tpu_custom_call" | custom-call | flops 2076180480 | bytes 10485760 | tf_op jit(solution)/shard_map/pallas_call | solution.py:238
  205.4 1.3 collective-permute-start.16
  207.8 6.2 %collective-permute-done.16.refs_3_ = bf16[880,128]{1,0:T(8,128)(2,1)S(1)} collective-permute-done((bf16[880,128]{1,0:T(8,128)(2,1)}, bf16[880,128]{1,0:T(8,128)(2,1)S(1)}, u32[]{:S(2)}, u32[]{:S(2)}) %collective-permute-start.16) | collective-permute-done | bytes 225312 | tf_op jit(solution)/shard_map/ppermute | solution.py:266
  214.7 6.7 %shard_map.119 = (bf16[784,128]{1,0:T(8,128)(2,1)}, bf16[512,128]{1,0:T(8,128)(2,1)}, bf16[512,512]{1,0:T(8,128)(2,1)}, f32[784,128]{1,0:T(8,128)}, f32[784,128]{1,0:T(8,128)}) custom-call(s32[1]{0:T(128)} %bitcast.refs_0_, bf16[1536,768]{1,0:T(8,128)(2,1)} %bitcast.92, f32[1360,768]{1,0:T(8,128)} %copy-done, bf16[880,128]{1,0:T(8,128)(2,1)} %copy-done.31, ...), custom_call_target="tpu_custom_call" | custom-call | flops 1849688064 | bytes 10485760 | tf_op jit(solution)/shard_map/pallas_call | solution.py:238
  221.4 1.2 bitcast_dynamic-update-slice_fusion
  223.4 31.3 %fusion.18 = bf16[2304,512]{1,0:T(8,128)(2,1)} fusion(bf16[1536,512]{1,0:T(8,128)(2,1)S(1)} %bitcast.110, bf16[512,768]{1,0:T(8,128)(2,1)S(1)} %bitcast.118, bf16[512,768]{1,0:T(8,128)(2,1)S(1)} %bitcast.119, bf16[512,768]{1,0:T(8,128)(2,1)S(1)} %bitcast.117, bf16[512,768]{1,0:T(8,128)(2,1)} %bitcast.121, bf16[512,768]{1,0:T(8,128)(2,1)} %bitcast.122, ...), kind=kOutput, calls=%fused_computation.19 | convolution fusion | flops 3688759296 | bytes 11010048 | tf_op jit(solution)/shard_map/dot_general | solution.py:272
  254.7 18.5 %all-to-all-start.1 = ((bf16[32,72,512]{2,1,0:T(8,128)(2,1)}), bf16[32,72,512]{2,1,0:T(8,128)(2,1)S(1)}, u32[]{:S(2)}, u32[]{:S(2)}) async-start(bf16[32,72,512]{2,1,0:T(8,128)(2,1)} %bitcast.109), calls=%async_computation.1 | async-start | bytes 4718592 | tf_op jit(solution)/shard_map/all_to_all | solution.py:275
  275.2 27.0 %all-to-all-done.1 = bf16[32,72,512]{2,1,0:T(8,128)(2,1)S(1)} async-done(((bf16[32,72,512]{2,1,0:T(8,128)(2,1)}), bf16[32,72,512]{2,1,0:T(8,128)(2,1)S(1)}, u32[]{:S(2)}, u32[]{:S(2)}) %all-to-all-start.1) | async-done | bytes 2359328 | tf_op jit(solution)/shard_map/all_to_all | solution.py:275
  (128 shorter events, 33.9 us)
Async XLA Ops:
  3.2 10.7 %copy-start.18 = (bf16[3,1,16,32,128]{4,3,2,1,0:T(8,128)(2,1)S(1)}, bf16[3,1,16,32,128]{4,3,2,1,0:T(8,128)(2,1)}, u32[]{:S(2)}) copy-start(bf16[3,1,16,32,128]{4,3,2,1,0:T(8,128)(2,1)} %param.11) | copy-start | bytes 1179652
  3.2 10.7 %copy-start.19 = (bf16[1,3,1,16,32,128]{5,4,3,2,1,0:T(8,128)(2,1)S(1)}, bf16[1,3,1,16,32,128]{5,4,3,2,1,0:T(8,128)(2,1)}, u32[]{:S(2)}) copy-start(bf16[1,3,1,16,32,128]{5,4,3,2,1,0:T(8,128)(2,1)} %param.9) | copy-start | bytes 1179652
  3.2 10.7 %copy-start.20 = (bf16[1,3,1,16,32,128]{5,4,3,2,1,0:T(8,128)(2,1)S(1)}, bf16[1,3,1,16,32,128]{5,4,3,2,1,0:T(8,128)(2,1)}, u32[]{:S(2)}) copy-start(bf16[1,3,1,16,32,128]{5,4,3,2,1,0:T(8,128)(2,1)} %param.8) | copy-start | bytes 1179652
  3.2 90.8 %all-to-all-start = ((bf16[32,72,512]{2,1,0:T(8,128)(2,1)}), bf16[32,72,512]{2,1,0:T(8,128)(2,1)S(1)}, u32[]{:S(2)}, u32[]{:S(2)}) async-start(bf16[32,72,512]{2,1,0:T(8,128)(2,1)} %tile.2), calls=%async_computation | async-start | bytes 4718592 | tf_op jit(solution)/shard_map/all_to_all | solution.py:173
  14.9 51.2 %collective-permute-start.1 = (bf16[7,32,512]{2,1,0:T(8,128)(2,1)}, bf16[7,32,512]{2,1,0:T(8,128)(2,1)}, u32[]{:S(2)}, u32[]{:S(2)}) collective-permute-start(bf16[7,32,512]{2,1,0:T(8,128)(2,1)} %get-tuple-element.86), channel_id=1, source_target_pairs={{8,0},{9,1},{10,2},{11,3},{12,4},{13,5},{14,6},{15,7},{16,8},{17,9... | collective-permute-start | bytes 688136 | tf_op jit(solution)/shard_map/ppermute | solution.py:184
  17.0 34.5 %collective-permute-start.10 = (bf16[5,32,512]{2,1,0:T(8,128)(2,1)}, bf16[5,32,512]{2,1,0:T(8,128)(2,1)}, u32[]{:S(2)}, u32[]{:S(2)}) collective-permute-start(bf16[5,32,512]{2,1,0:T(8,128)(2,1)} %get-tuple-element.79), channel_id=1, source_target_pairs={{8,0},{9,1},{10,2},{11,3},{12,4},{13,5},{14,6},{15,7},{16,8},{17,9... | collective-permute-start | bytes 491528 | tf_op jit(solution)/shard_map/ppermute | solution.py:184
  18.3 38.7 %collective-permute-start.9 = (bf16[5,32,512]{2,1,0:T(8,128)(2,1)}, bf16[5,32,512]{2,1,0:T(8,128)(2,1)}, u32[]{:S(2)}, u32[]{:S(2)}) collective-permute-start(bf16[5,32,512]{2,1,0:T(8,128)(2,1)} %get-tuple-element.78), channel_id=1, source_target_pairs={{0,8},{1,9},{2,10},{3,11},{4,12},{5,13},{6,14},{7,15},{8,16},{9,17... | collective-permute-start | bytes 491528 | tf_op jit(solution)/shard_map/ppermute | solution.py:183
  26.4 32.8 %collective-permute-start.5 = (bf16[6,32,512]{2,1,0:T(8,128)(2,1)}, bf16[6,32,512]{2,1,0:T(8,128)(2,1)}, u32[]{:S(2)}, u32[]{:S(2)}) collective-permute-start(bf16[6,32,512]{2,1,0:T(8,128)(2,1)} %get-tuple-element.84), channel_id=1, source_target_pairs={{8,0},{9,1},{10,2},{11,3},{12,4},{13,5},{14,6},{15,7},{16,8},{17,9... | collective-permute-start | bytes 589832 | tf_op jit(solution)/shard_map/ppermute | solution.py:184
  27.7 36.1 %collective-permute-start.4 = (bf16[6,32,512]{2,1,0:T(8,128)(2,1)}, bf16[6,32,512]{2,1,0:T(8,128)(2,1)}, u32[]{:S(2)}, u32[]{:S(2)}) collective-permute-start(bf16[6,32,512]{2,1,0:T(8,128)(2,1)} %get-tuple-element.83), channel_id=1, source_target_pairs={{0,8},{1,9},{2,10},{3,11},{4,12},{5,13},{6,14},{7,15},{8,16},{9,17... | collective-permute-start | bytes 589832 | tf_op jit(solution)/shard_map/ppermute | solution.py:183
  51.5 19.3 %collective-permute-start = (bf16[7,32,512]{2,1,0:T(8,128)(2,1)}, bf16[7,32,512]{2,1,0:T(8,128)(2,1)S(1)}, u32[]{:S(2)}, u32[]{:S(2)}) collective-permute-start(bf16[7,32,512]{2,1,0:T(8,128)(2,1)} %get-tuple-element.85), channel_id=1, source_target_pairs={{0,8},{1,9},{2,10},{3,11},{4,12},{5,13},{6,14},{7,15},{8,16},{9,17... | collective-permute-start | bytes 688136 | tf_op jit(solution)/shard_map/ppermute | solution.py:183
  57.9 15.0 %collective-permute-start.12 = (bf16[26,8,512]{2,1,0:T(8,128)(2,1)S(1)}, bf16[26,8,512]{2,1,0:T(8,128)(2,1)S(1)}, u32[]{:S(2)}, u32[]{:S(2)}) collective-permute-start(bf16[26,8,512]{2,1,0:T(8,128)(2,1)S(1)} %get-tuple-element.98), channel_id=1, source_target_pairs={{1,0},{2,1},{3,2},{4,3},{5,4},{6,5},{7,6},{9,8},{10,9},{11,10},{12... | collective-permute-start | bytes 638984 | tf_op jit(solution)/shard_map/ppermute | solution.py:187
  59.2 18.4 %collective-permute-start.11 = (bf16[26,8,512]{2,1,0:T(8,128)(2,1)S(1)}, bf16[26,8,512]{2,1,0:T(8,128)(2,1)S(1)}, u32[]{:S(2)}, u32[]{:S(2)}) collective-permute-start(bf16[26,8,512]{2,1,0:T(8,128)(2,1)S(1)} %get-tuple-element.97), channel_id=1, source_target_pairs={{0,1},{1,2},{2,3},{3,4},{4,5},{5,6},{6,7},{8,9},{9,10},{10,11},{11... | collective-permute-start | bytes 638984 | tf_op jit(solution)/shard_map/ppermute | solution.py:186
  64.8 15.2 %collective-permute-start.7 = (bf16[28,8,512]{2,1,0:T(8,128)(2,1)S(1)}, bf16[28,8,512]{2,1,0:T(8,128)(2,1)S(1)}, u32[]{:S(2)}, u32[]{:S(2)}) collective-permute-start(bf16[28,8,512]{2,1,0:T(8,128)(2,1)S(1)} %get-tuple-element.96), channel_id=1, source_target_pairs={{1,0},{2,1},{3,2},{4,3},{5,4},{6,5},{7,6},{9,8},{10,9},{11,10},{12... | collective-permute-start | bytes 688136 | tf_op jit(solution)/shard_map/ppermute | solution.py:187
  66.1 13.9 %collective-permute-start.6 = (bf16[28,8,512]{2,1,0:T(8,128)(2,1)S(1)}, bf16[28,8,512]{2,1,0:T(8,128)(2,1)S(1)}, u32[]{:S(2)}, u32[]{:S(2)}) collective-permute-start(bf16[28,8,512]{2,1,0:T(8,128)(2,1)S(1)} %get-tuple-element.95), channel_id=1, source_target_pairs={{0,1},{1,2},{2,3},{3,4},{4,5},{5,6},{6,7},{8,9},{9,10},{10,11},{11... | collective-permute-start | bytes 688136 | tf_op jit(solution)/shard_map/ppermute | solution.py:186
  71.6 16.6 %collective-permute-start.3 = (bf16[30,8,512]{2,1,0:T(8,128)(2,1)S(1)}, bf16[30,8,512]{2,1,0:T(8,128)(2,1)S(1)}, u32[]{:S(2)}, u32[]{:S(2)}) collective-permute-start(bf16[30,8,512]{2,1,0:T(8,128)(2,1)S(1)} %get-tuple-element.94), channel_id=1, source_target_pairs={{1,0},{2,1},{3,2},{4,3},{5,4},{6,5},{7,6},{9,8},{10,9},{11,10},{12... | collective-permute-start | bytes 737288 | tf_op jit(solution)/shard_map/ppermute | solution.py:187
  72.9 7.1 %copy-start.17 = (bf16[16,32,512]{2,1,0:T(8,128)(2,1)S(1)}, bf16[16,32,512]{2,1,0:T(8,128)(2,1)}, u32[]{:S(2)}) copy-start(bf16[16,32,512]{2,1,0:T(8,128)(2,1)} %get-tuple-element.81) | copy-start | bytes 1572868
  72.9 15.3 %collective-permute-start.2 = (bf16[30,8,512]{2,1,0:T(8,128)(2,1)S(1)}, bf16[30,8,512]{2,1,0:T(8,128)(2,1)S(1)}, u32[]{:S(2)}, u32[]{:S(2)}) collective-permute-start(bf16[30,8,512]{2,1,0:T(8,128)(2,1)S(1)} %get-tuple-element.93), channel_id=1, source_target_pairs={{0,1},{1,2},{2,3},{3,4},{4,5},{5,6},{6,7},{8,9},{9,10},{10,11},{11... | collective-permute-start | bytes 737288 | tf_op jit(solution)/shard_map/ppermute | solution.py:186
  83.2 1.4 copy-start.14
  84.7 2.1 copy-start.15
  91.1 1.4 copy-start.16
  94.0 3.9 %copy-start.13 = (bf16[32,72,512]{2,1,0:T(8,128)(2,1)}, bf16[32,72,512]{2,1,0:T(8,128)(2,1)S(1)}, u32[]{:S(2)}) copy-start(bf16[32,72,512]{2,1,0:T(8,128)(2,1)S(1)} %all-to-all-done) | copy-start | bytes 7077892
  104.6 2.0 copy-start.2
  110.9 0.8 copy-start.3
  111.7 0.8 copy-start.4
  112.6 10.7 %collective-permute-start.8 = (bf16[1264,128]{1,0:T(8,128)(2,1)}, bf16[1264,128]{1,0:T(8,128)(2,1)S(1)}, u32[]{:S(2)}, u32[]{:S(2)}) collective-permute-start(bf16[1264,128]{1,0:T(8,128)(2,1)} %get-tuple-element.32), channel_id=1, source_target_pairs={{96,64},{97,65},{98,66},{99,67},{100,68},{101,69},{102,70},{103,71... | collective-permute-start | bytes 970760 | tf_op jit(solution)/shard_map/ppermute | solution.py:266
  121.3 1.9 copy-start.1
  129.8 0.8 copy-start.5
  130.7 0.8 copy-start.6
  131.5 9.3 %collective-permute-start.13 = (bf16[1168,128]{1,0:T(8,128)(2,1)}, bf16[1168,128]{1,0:T(8,128)(2,1)S(1)}, u32[]{:S(2)}, u32[]{:S(2)}) collective-permute-start(bf16[1168,128]{1,0:T(8,128)(2,1)} %get-tuple-element.36), channel_id=1, source_target_pairs={{64,32},{96,64},{65,33},{97,65},{66,34},{98,66},{67,35},{99,67},{6... | collective-permute-start | bytes 897032 | tf_op jit(solution)/shard_map/ppermute | solution.py:266
  138.9 1.9 copy-start
  141.5 10.0 %copy-start.26 = (bf16[512,512]{1,0:T(8,128)(2,1)S(1)}, bf16[512,512]{1,0:T(8,128)(2,1)}, u32[]{:S(2)}) copy-start(bf16[512,512]{1,0:T(8,128)(2,1)} %get-tuple-element.53) | copy-start | bytes 1572868
  148.6 0.8 copy-start.7
  150.2 10.2 %collective-permute-start.14 = (bf16[1072,128]{1,0:T(8,128)(2,1)}, bf16[1072,128]{1,0:T(8,128)(2,1)S(1)}, u32[]{:S(2)}, u32[]{:S(2)}) collective-permute-start(bf16[1072,128]{1,0:T(8,128)(2,1)} %get-tuple-element.40), channel_id=1, source_target_pairs={{32,0},{64,32},{96,64},{33,1},{65,33},{97,65},{34,2},{66,34},{98,6... | collective-permute-start | bytes 823304 | tf_op jit(solution)/shard_map/ppermute | solution.py:266
  184.6 10.6 %collective-permute-start.15 = (bf16[976,128]{1,0:T(8,128)(2,1)}, bf16[976,128]{1,0:T(8,128)(2,1)S(1)}, u32[]{:S(2)}, u32[]{:S(2)}) collective-permute-start(bf16[976,128]{1,0:T(8,128)(2,1)} %get-tuple-element.44), channel_id=1, source_target_pairs={{32,0},{64,32},{33,1},{65,33},{34,2},{66,34},{35,3},{67,35},{36,4}... | collective-permute-start | bytes 749576 | tf_op jit(solution)/shard_map/ppermute | solution.py:266
  205.4 8.6 %collective-permute-start.16 = (bf16[880,128]{1,0:T(8,128)(2,1)}, bf16[880,128]{1,0:T(8,128)(2,1)S(1)}, u32[]{:S(2)}, u32[]{:S(2)}) collective-permute-start(bf16[880,128]{1,0:T(8,128)(2,1)} %get-tuple-element.48), channel_id=1, source_target_pairs={{32,0},{33,1},{34,2},{35,3},{36,4},{37,5},{38,6},{39,7},{40,8},{41... | collective-permute-start | bytes 675848 | tf_op jit(solution)/shard_map/ppermute | solution.py:266
  221.4 1.4 copy-start.21
  221.4 1.5 copy-start.22
  221.4 1.8 copy-start.23
  221.4 2.0 copy-start.24
  254.7 18.5 %copy-start.34 = (bf16[512,128]{1,0:T(8,128)(2,1)S(1)}, bf16[512,128]{1,0:T(8,128)(2,1)}, u32[]{:S(2)}) copy-start(bf16[512,128]{1,0:T(8,128)(2,1)} %get-tuple-element.31) | copy-start | bytes 393220
  254.7 18.5 %copy-start.35 = (bf16[512,128]{1,0:T(8,128)(2,1)S(1)}, bf16[512,128]{1,0:T(8,128)(2,1)}, u32[]{:S(2)}) copy-start(bf16[512,128]{1,0:T(8,128)(2,1)} %get-tuple-element.35) | copy-start | bytes 393220
  254.7 18.6 %copy-start.36 = (bf16[512,128]{1,0:T(8,128)(2,1)S(1)}, bf16[512,128]{1,0:T(8,128)(2,1)}, u32[]{:S(2)}) copy-start(bf16[512,128]{1,0:T(8,128)(2,1)} %get-tuple-element.39) | copy-start | bytes 393220
  254.7 18.6 %copy-start.37 = (bf16[512,128]{1,0:T(8,128)(2,1)S(1)}, bf16[512,128]{1,0:T(8,128)(2,1)}, u32[]{:S(2)}) copy-start(bf16[512,128]{1,0:T(8,128)(2,1)} %get-tuple-element.43) | copy-start | bytes 393220
  254.7 18.7 %copy-start.38 = (bf16[512,128]{1,0:T(8,128)(2,1)S(1)}, bf16[512,128]{1,0:T(8,128)(2,1)}, u32[]{:S(2)}) copy-start(bf16[512,128]{1,0:T(8,128)(2,1)} %get-tuple-element.47) | copy-start | bytes 393220
  254.7 47.5 %all-to-all-start.1 = ((bf16[32,72,512]{2,1,0:T(8,128)(2,1)}), bf16[32,72,512]{2,1,0:T(8,128)(2,1)S(1)}, u32[]{:S(2)}, u32[]{:S(2)}) async-start(bf16[32,72,512]{2,1,0:T(8,128)(2,1)} %bitcast.109), calls=%async_computation.1 | async-start | bytes 4718592 | tf_op jit(solution)/shard_map/all_to_all | solution.py:275
  273.3 29.3 %copy-start.25 = (f32[1,72,512]{2,1,0:T(8,128)S(1)}, f32[1,72,512]{2,1,0:T(8,128)}, u32[]{:S(2)}) copy-start(f32[1,72,512]{2,1,0:T(8,128)} %param.13) | copy-start | bytes 442372
  273.3 29.3 %copy-start.32 = (f32[1,72,512]{2,1,0:T(8,128)S(1)}, f32[1,72,512]{2,1,0:T(8,128)}, u32[]{:S(2)}) copy-start(f32[1,72,512]{2,1,0:T(8,128)} %param.14) | copy-start | bytes 442372
  273.3 29.3 %copy-start.33 = (f32[1,72,512]{2,1,0:T(8,128)S(1)}, f32[1,72,512]{2,1,0:T(8,128)}, u32[]{:S(2)}) copy-start(f32[1,72,512]{2,1,0:T(8,128)} %param.15) | copy-start | bytes 442372
  (10 other events, 7.5 us)
where the time goes:
time: 307 us; the launch traced here: 304 us
  starting transfers between devices  74.8 us (24%)
  Pallas kernels  73.9 us (24%)
  waiting for transfers between devices  65.2 us (21%)
  local copies, waits for them, and re-layouts  45.7 us (15%)
  matrix products  31.3 us (10%)
  other arithmetic  11.2 us (4%)
    pallas_call x6, Pallas kernels, on_device(): pl.pallas_call(functools.partial(step_kernel, step, layers, frames, pitch...  53.7 us
    dot_general x1, matrix products, on_device(): lax.dot_general(all_patches, flat_dgates, (((0,), (0,)), ((), ())), prefe...  31.3 us
    all_to_all x1, waiting for transfers between devices, on_device(): arrived = lax.all_to_all(partial, 'tile', 0, 0, tiled=True)  27 us
    unnamed x88, local copies, waits for them, and re-layouts  24.9 us
    ppermute x5, waiting for transfers between devices, on_device(): state = [lax.ppermute(dx, 'section', pairs), dh_rec, dc_rec]  22.3 us
    pallas_call x3, Pallas kernels, on_device(): pl.pallas_call(functools.partial(gates_kernel, pitch, size_d, width), out...  20.2 us
    ppermute x3, starting transfers between devices, on_device(): lax.ppermute(block[rows - deep:], 'tile', row_pairs(ntile, ncols, 1))  19.9 us
    all_to_all x1, starting transfers between devices, on_device(): arrived = lax.all_to_all(partial, 'tile', 0, 0, tiled=True)  18.5 us
  transfers between devices with their start and end apart: 19, of which 5 were waited for; matrix products, arithmetic and copies ran while one was open for 9% of the time, Pallas kernels for 4%

commit v1 on v0

--- a/solution.py
+++ b/solution.py
@@ -12,7 +12,10 @@
 F32 = jnp.float32
 SIDE = 8
 LEAD = 16
-VMEM_LIMIT = 56 * 1024 * 1024
+
+
+def params(mib):
+    return pltpu.CompilerParams(vmem_limit_bytes=mib << 20)
 
 
 def chunks(size, most):
@@ -62,7 +65,7 @@
 
 def step_kernel(step, layers, frames, pitch, rows, cols, width, *refs):
     ids_ref, kernel_t_ref = refs[0], refs[1]
-    picks = [f for f in range(frames) if 0 <= frames - 1 - step + layers - 1 - f <= layers - 1]
+    picks = picks_of(step, layers, frames)
     fac_refs = refs[2 : 2 + len(picks)]
     at = 2 + len(picks)
     first, tops = step == 0, step < frames
@@ -70,7 +73,7 @@
     at += 1 if tops else 0
     if not first:
         inc_ref, dh_ref, dc_ref = refs[at : at + 3]
-        at += 3
+        at += 5
     dx_ref, dxi_ref, dgi_ref, dhn_ref, dcn_ref, d_ref, p_ref = refs[at:]
     margin = frames + layers - 1 - step
     size_d = LEAD + (rows + 2 * margin) * pitch
@@ -84,8 +87,7 @@
             here = pl.ds(start, size)
             there = pl.ds(start + step * pitch, size)
             if tops and pick == top_frame:
-                own = ext_ref[pl.ds(start + (step + 1) * pitch, size), 3 * width :]
-                above = own.astype(F32)
+                above = ext_ref[pl.ds(start + (step + 1) * pitch, size), 3 * width :].astype(F32)
             else:
                 above = inc_ref[here, :].astype(F32)
             dh = above
@@ -109,15 +111,13 @@
 
     @pl.when((frame >= 0) & (frame < frames))
     def _():
+        slot = pl.multiple_of(frame * (rows * cols), rows * cols)
         for row in range(rows):
-            dgi_ref[row * cols : (row + 1) * cols, :] = d_ref[
+            dgi_ref[pl.ds(slot + row * cols, cols), :] = d_ref[
                 pl.ds(LEAD + (row + margin) * pitch, cols), :
             ]
-        for side in range(3):
-            p_ref[0:8, side * 2 * width : (side + 1) * 2 * width] = jnp.zeros((8, 2 * width), F32)
-            p_ref[8 + size_z : 16 + size_z, side * 2 * width : (side + 1) * 2 * width] = jnp.zeros(
-                (8, 2 * width), F32
-            )
+        p_ref[0:8, :] = jnp.zeros((8, 6 * width), F32)
+        p_ref[8 + size_z : 16 + size_z, :] = jnp.zeros((8, 6 * width), F32)
         for start, size in chunks(size_z, 448):
             total = None
             for a in range(3):
@@ -137,25 +137,46 @@
             dx_ref[pl.ds(start, size), :] = dz[:, :width].astype(BF)
             dhn_ref[pl.ds(start, size), :] = dz[:, width:]
         for row in range(rows):
-            dxi_ref[row * cols : (row + 1) * cols, :] = dx_ref[
+            dxi_ref[pl.ds(slot + row * cols, cols), :] = dx_ref[
                 pl.ds(LEAD + (row + margin - 1) * pitch, cols), :
             ]
 
 
+def picks_of(step, layers, frames):
+    return [f for f in range(frames) if 0 <= frames - 1 - step + layers - 1 - f <= layers - 1]
+
+
+def patch_kernel(pitch, rows, cols, edge, zs_ref, pt_ref, flat_ref):
+    depth = zs_ref.shape[1]
+    for a in range(3):
+        for row in range(rows):
+            flat_ref[row * cols : (row + 1) * cols, :] = zs_ref[
+                pl.ds(LEAD + (edge + row + a) * pitch, cols), :
+            ]
+        pt_ref[a * depth : (a + 1) * depth, :] = flat_ref[...].T
+
+
+def grad_kernel(cells, frame, count, begin, end, *refs):
+    pts, dg_ref = refs[:count], refs[count]
+    total_ref = None if begin else refs[count + 1]
+    out_ref = refs[-1]
+    block = 256
+    for at in range(0, out_ref.shape[0], block):
+        here = pl.ds(at, block)
+        total = None if begin else total_ref[here, :]
+        part = jnp.dot(
+            pts[0][here, :], dg_ref[frame * cells : (frame + 1) * cells, :], preferred_element_type=F32
+        )
+        total = part if begin else total + part
+        out_ref[here, :] = total.astype(out_ref.dtype)
+
+
 def spec_v():
     return pl.BlockSpec(memory_space=pltpu.VMEM)
 
 
 def spec_s():
     return pl.BlockSpec(memory_space=pltpu.SMEM)
-
-
-def row_pairs(ntile, ncols, by):
-    return [(i, i + by * ncols) for i in range(ntile) if 0 <= i + by * ncols < ntile]
-
-
-def col_pairs(ntile, ncols, by):
-    return [(i, i + by) for i in range(ntile) if 0 <= i % ncols + by < ncols]
 
 
 def on_device(layer_input, hidden_prev, cell_prev, out_cot, bias, master, moment1, moment2):
@@ -176,48 +197,68 @@
     packed = jnp.concatenate(
         [layer_input[0, :, 0], hidden_prev[0, :, 0], cell_prev[0, :, 0].astype(BF), out_cot[:, 0]], -1
     )
-    ext = [None] * frames
-    for f in reversed(range(frames)):
-        deep = edge + 1 - (frames - 1 - f)
-        block = packed[f]
-        above = lax.ppermute(block[rows - deep :], "tile", row_pairs(ntile, ncols, 1))
-        below = lax.ppermute(block[:deep], "tile", row_pairs(ntile, ncols, -1))
-        tall = jnp.concatenate([above, block, below], 0)
-        left = lax.ppermute(tall[:, cols - SIDE :], "tile", col_pairs(ntile, ncols, 1))
-        right = lax.ppermute(tall[:, :SIDE], "tile", col_pairs(ntile, ncols, -1))
-        wide = jnp.concatenate([left, tall, right], 1)
-        gap = edge + 1 - deep
-        flat = wide.reshape(-1, 4 * width)
-        ext[f] = jnp.pad(
-            flat, ((LEAD - SIDE + gap * pitch, SIDE + gap * pitch), (0, 0))
+    deeps = [edge + 1 - (frames - 1 - f) for f in range(frames)]
+    grid_row, grid_col = tile // ncols, tile % ncols
+
+    def around(by, strip, keep):
+        got = lax.ppermute(strip, "tile", [(i, by(i)) for i in range(ntile)])
+        return jnp.where(keep, got, jnp.zeros_like(got))
+
+    downs = jnp.concatenate([packed[f, rows - deeps[f] :] for f in range(frames)], 0)
+    ups = jnp.concatenate([packed[f, : deeps[f]] for f in range(frames)], 0)
+    above = around(lambda i: (i + ncols) % ntile, downs, grid_row > 0)
+    below = around(lambda i: (i - ncols) % ntile, ups, grid_row < TILE_ROWS - 1)
+    talls, at = [], 0
+    for f in range(frames):
+        talls.append(jnp.concatenate([above[at : at + deeps[f]], packed[f], below[at : at + deeps[f]]], 0))
+        at += deeps[f]
+    rights = jnp.concatenate([t[:, cols - SIDE :] for t in talls], 0)
+    lefts = jnp.concatenate([t[:, :SIDE] for t in talls], 0)
+    left = around(lambda i: i // ncols * ncols + (i + 1) % ncols, rights, grid_col > 0)
+    right = around(lambda i: i // ncols * ncols + (i - 1) % ncols, lefts, grid_col < ncols - 1)
+    ext, at = [], 0
+    for f in range(frames):
+        tall = rows + 2 * deeps[f]
+        wide = jnp.concatenate([left[at : at + tall], talls[f], right[at : at + tall]], 1)
+        at += tall
+        gap = edge + 1 - deeps[f]
+        ext.append(
+            jnp.pad(
+                wide.reshape(-1, 4 * width), ((LEAD - SIDE + gap * pitch, SIDE + gap * pitch), (0, 0))
+            )
         )
     size_e = LEAD + (rows + 2 * edge + 2) * pitch
     size_d = LEAD + (rows + 2 * edge) * pitch
+    cells = rows * cols
 
     at = jnp.arange(size_d, dtype=jnp.int32) - LEAD + SIDE
-    row_at = at // pitch - edge + (tile // ncols) * rows
-    col_at = at % pitch - SIDE + (tile % ncols) * cols
+    row_at = at // pitch - edge + grid_row * rows
+    col_at = at % pitch - SIDE + grid_col * cols
     inside = (row_at >= 0) & (row_at < TILE_ROWS * rows) & (col_at >= 0) & (col_at < ncols * cols)
     mask = jnp.broadcast_to(inside[:, None], (size_d, width)).astype(BF)
 
-    params = pltpu.CompilerParams(vmem_limit_bytes=VMEM_LIMIT)
-    facs, patches = [None] * frames, [None] * frames
+    facs, pts = [None] * frames, [None] * frames
     for f in reversed(range(frames)):
         z = ext[f][:, : 2 * width]
         none = jnp.zeros((1, 2 * width), BF)
         zs = jnp.concatenate(
             [jnp.concatenate([none, z[:-1]], 0), z, jnp.concatenate([z[1:], none], 0)], -1
         )
-        inner = zs[LEAD:].reshape(rows + 2 * edge + 2, pitch, 6 * width)[edge : edge + rows + 2, :cols]
-        patches[f] = jnp.concatenate(
-            [inner[a : a + rows].reshape(rows * cols, 6 * width) for a in range(3)], -1
-        )
+        pts[f] = pl.pallas_call(
+            functools.partial(patch_kernel, pitch, rows, cols, edge),
+            out_shape=in_vmem((18 * width, cells), BF),
+            in_specs=[spec_v()],
+            out_specs=spec_v(),
+            scratch_shapes=[pltpu.VMEM((cells, 6 * width), BF)],
+            compiler_params=params(16),
+            cost_estimate=pl.CostEstimate(flops=0, bytes_accessed=8 << 20, transcendentals=0),
+        )(zs)
         facs[f] = pl.pallas_call(
             functools.partial(gates_kernel, pitch, size_d, width),
             out_shape=in_vmem((size_d, 6 * width), F32),
             in_specs=[spec_v()] * 5,
             out_specs=spec_v(),
-            compiler_params=params,
+            compiler_params=params(16),
             cost_estimate=pl.CostEstimate(
                 flops=2 * size_d * 18 * width * ngate, bytes_accessed=10 << 20, transcendentals=size_d * 5 * width
             ),
@@ -225,22 +266,21 @@
 
     ids = (frames - 1 + layers - 1 - layer).astype(jnp.int32).reshape(1)
     state = []
-    sent_dx, kept = [], []
     steps = layers + frames - 1
+    total = None
     for step in range(steps):
         margin = edge - step
         size_z = LEAD + (rows + 2 * margin - 2) * pitch
-        picks = [f for f in range(frames) if 0 <= frames - 1 - step + layers - 1 - f <= layers - 1]
-        args = [ids, kernel_t] + [facs[f] for f in picks]
+        args = [ids, kernel_t] + [facs[f] for f in picks_of(step, layers, frames)]
         if step < frames:
             args.append(ext[frames - 1 - step])
         args += state
-        dx, dxi, dgi, dh_rec, dc_rec = pl.pallas_call(
+        dx, cots, dgates, dh_rec, dc_rec = pl.pallas_call(
             functools.partial(step_kernel, step, layers, frames, pitch, rows, cols, width),
             out_shape=(
                 jax.ShapeDtypeStruct((size_z, width), BF),
-                jax.ShapeDtypeStruct((rows * cols, width), BF),
-                jax.ShapeDtypeStruct((rows * cols, ngate), BF),
+                in_vmem((frames * cells, width), BF),
+                in_vmem((frames * cells, ngate), BF),
                 in_vmem((size_z, width), F32),
                 in_vmem((size_z, width), F32),
             ),
@@ -250,31 +290,38 @@
                 pltpu.VMEM((size_z + 2 * pitch, ngate), BF),
                 pltpu.VMEM((size_z + 16, 6 * width), F32),
             ],
-            compiler_params=params,
+            input_output_aliases={len(args) - 2: 1, len(args) - 1: 2} if step else {},
+            compiler_params=params(20),
             cost_estimate=pl.CostEstimate(
                 flops=2 * size_z * 18 * width * ngate, bytes_accessed=10 << 20, transcendentals=0
             ),
         )(*args)
-        sent_dx.append(dxi)
-        kept.append(dgi)
         if step < steps - 1:
             pairs = [
                 (i, i - 1)
                 for i in range(1, layers)
                 if 0 <= frames - 1 - step + layers - 1 - i < frames
             ]
-            state = [lax.ppermute(dx, "section", pairs), dh_rec, dc_rec]
-
-    first = layers - 1 - layer
-    late = lax.dynamic_slice_in_dim(jnp.stack(kept), first, frames, 0)
-    flat_dgates = late.reshape(frames * rows * cols, ngate)
-    all_patches = jnp.concatenate([patches[f] for f in reversed(range(frames))], 0)
-    partial = lax.dot_general(
-        all_patches, flat_dgates, (((0,), (0,)), ((), ())), preferred_element_type=F32
-    ).astype(BF)
-    arrived = lax.all_to_all(partial, "tile", 0, 0, tiled=True)
-    cots = lax.dynamic_slice_in_dim(jnp.stack(sent_dx), first, frames, 0)
-    input_cot = jnp.flip(cots, 0).reshape(frames, rows, cols, width)
+            state = [lax.ppermute(dx, "section", pairs), dh_rec, dc_rec, cots, dgates]
+        if step >= layers - 1:
+            f = frames - 1 - (step - layers + 1)
+            end = step == steps - 1
+            args = [pts[f], dgates] + ([] if total is None else [total])
+            total = pl.pallas_call(
+                functools.partial(grad_kernel, cells, f, 1, total is None, end),
+                out_shape=jax.ShapeDtypeStruct((18 * width, ngate), BF) if end else in_vmem((18 * width, ngate), F32),
+                in_specs=[spec_v()] * len(args),
+                out_specs=spec_v(),
+                compiler_params=params(16),
+                cost_estimate=pl.CostEstimate(
+                    flops=2 * cells * 18 * width * ngate, bytes_accessed=4 << 20, transcendentals=0
+                ),
+            )(*args)
+
+    total, cots = lax.optimization_barrier((total, cots))
+    arrived = lax.all_to_all(total, "tile", 0, 0, tiled=True)
+    arrived, cots = lax.optimization_barrier((arrived, cots))
+    input_cot = cots.reshape(frames, rows, cols, width)
     grad_rows = jnp.sum(arrived.reshape(ntile, -1, ngate).astype(F32), 0)
     new_moment1 = 0.9 * moment1[0] + 0.1 * grad_rows
     new_moment2 = 0.999 * moment2[0] + 0.001 * grad_rows * grad_rows

time: 307 us -> 203 us (0.66)
  starting transfers between devices: 74.8 us -> 20.7 us
  Pallas kernels: 73.9 us -> 26.7 us
  blocking collectives: 0 us -> 44.2 us
  matrix products: 31.3 us -> 0 us
  local copies, waits for them, and re-layouts: 45.7 us -> 20.9 us
  waiting for transfers between devices: 65.2 us -> 74.4 us
    pallas_call x6, Pallas kernels: 53.7 us -> 8.81 us  [on_device(): pl.pallas_call(functools.partial(step_kernel, step, layers, frames, pitch...]
    all_to_all x0 -> x1, blocking collectives: none -> 44.2 us  [on_device(): arrived = lax.all_to_all(total, 'tile', 0, 0, tiled=True)]
    ppermute x17 -> x9, waiting for transfers between devices: 38.2 us -> 74.4 us  [the longest x4 51.8 us: around(): got = lax.ppermute(strip, 'tile', [(i, by(i)) for i in range(ntile)])]
    ppermute x17 -> x9, starting transfers between devices: 46.8 us -> 14.6 us  [the longest x4 9.09 us: around(): got = lax.ppermute(strip, 'tile', [(i, by(i)) for i in range(ntile)])]
    dot_general x1 -> x0, matrix products: 31.3 us -> none  [on_device(): lax.dot_general(all_patches, flat_dgates, (((0,), (0,)), ((), ())), prefe...]
    all_to_all x1 -> x0, waiting for transfers between devices: 27 us -> none  [on_device(): arrived = lax.all_to_all(partial, 'tile', 0, 0, tiled=True)]
    all_to_all x1 -> x0, starting transfers between devices: 18.5 us -> none  [on_device(): arrived = lax.all_to_all(partial, 'tile', 0, 0, tiled=True)]
    unnamed x88 -> x77, local copies, waits for them, and re-layouts: 24.9 us -> 11.4 us
  transfers between devices with their start and end apart: 19 -> 10, of which waited for: 5 -> 7; matrix products, arithmetic and copies ran while one was open for 9% -> 6% of each run, Pallas kernels for 4% -> 6%
where the time goes in v1:
time: 203 us; the launch traced here: 202 us
  waiting for transfers between devices  74.4 us (37%)
  blocking collectives  44.2 us (22%)
  Pallas kernels  26.7 us (13%)
  local copies, waits for them, and re-layouts  20.9 us (10%)
  starting transfers between devices  20.7 us (10%)
  other arithmetic  13.9 us (7%)
    ppermute x4, waiting for transfers between devices, around(): got = lax.ppermute(strip, 'tile', [(i, by(i)) for i in range(ntile)])  51.8 us
    all_to_all x1, blocking collectives, on_device(): arrived = lax.all_to_all(total, 'tile', 0, 0, tiled=True)  44.2 us
    ppermute x5, waiting for transfers between devices, on_device(): state = [lax.ppermute(dx, 'section', pairs), dh_rec, dc_rec, cots, dgates]  22.7 us
    pallas_call x3, Pallas kernels, on_device(): pl.pallas_call(functools.partial(gates_kernel, pitch, size_d, width), out...  11.7 us
    unnamed x77, local copies, waits for them, and re-layouts  11.4 us
    ppermute x4, starting transfers between devices, around(): got = lax.ppermute(strip, 'tile', [(i, by(i)) for i in range(ntile)])  9.09 us
    pallas_call x6, Pallas kernels, on_device(): pl.pallas_call(functools.partial(step_kernel, step, layers, frames, pitch...  8.81 us
    all_to_all x1, starting transfers between devices, on_device(): lax.all_to_all(jnp.tile(own_rows, (ntile, 1)), 'tile', 0, 0, tiled=True)  6.03 us
  transfers between devices with their start and end apart: 10, of which 7 were waited for; matrix products, arithmetic and copies ran while one was open for 6% of the time, Pallas kernels for 6%

profile of v1, /device:TPU:0, one launch (start us, length us, event | category | flops | bytes accessed | tf_op | source)
XLA Modules:
  0.0 202.2 jit_solution(2890259277730337371)
XLA Ops:
  0.6 1.2 fusion.16
  1.9 1.5 pad_maximum_fusion
  3.5 0.9 pad_maximum_fusion.16
  4.4 4.0 %collective-permute-start = (bf16[18,32,512]{2,1,0:T(8,128)(2,1)}, bf16[18,32,512]{2,1,0:T(8,128)(2,1)}, u32[]{:S(2)}, u32[]{:S(2)}) collective-permute-start(bf16[18,32,512]{2,1,0:T(8,128)(2,1)} %pad_maximum_fusion.16), channel_id=1, source_target_pairs={{0,8},{1,9},{2,10},{3,11},{4,12},{5,13},{6,14},{7,15},{8,16},{9,17... | collective-permute-start | bytes 1769480 | tf_op jit(solution)/shard_map/ppermute | solution.py:204
  8.5 0.9 pad_maximum_fusion.17
  9.4 0.9 collective-permute-start.1
  10.5 23.5 %collective-permute-done = bf16[18,32,512]{2,1,0:T(8,128)(2,1)} collective-permute-done((bf16[18,32,512]{2,1,0:T(8,128)(2,1)}, bf16[18,32,512]{2,1,0:T(8,128)(2,1)}, u32[]{:S(2)}, u32[]{:S(2)}) %collective-permute-start) | collective-permute-done | bytes 589856 | tf_op jit(solution)/shard_map/ppermute | solution.py:204
  34.1 1.5 collective-permute-done.1
  35.6 1.1 broadcast_select_fusion.2
  36.8 1.3 fusion.14
  38.1 1.6 collective-permute-start.2
  39.8 2.6 %collective-permute-start.3 = (bf16[84,8,512]{2,1,0:T(8,128)(2,1)}, bf16[84,8,512]{2,1,0:T(8,128)(2,1)}, u32[]{:S(2)}, u32[]{:S(2)}) collective-permute-start(bf16[84,8,512]{2,1,0:T(8,128)(2,1)} %get-tuple-element.78), channel_id=1, source_target_pairs={{0,7},{1,0},{2,1},{3,2},{4,3},{5,4},{6,5},{7,6},{8,15},{9,8},{10,9... | collective-permute-start | bytes 2064392 | tf_op jit(solution)/shard_map/ppermute | solution.py:204
  42.3 1.6 tile.2
  43.9 6.0 %all-to-all-start = ((bf16[32,72,512]{2,1,0:T(8,128)(2,1)}), bf16[32,72,512]{2,1,0:T(8,128)(2,1)S(1)}, u32[]{:S(2)}, u32[]{:S(2)}) async-start(bf16[32,72,512]{2,1,0:T(8,128)(2,1)} %tile.2), calls=%async_computation | async-start | bytes 4718592 | tf_op jit(solution)/shard_map/all_to_all | solution.py:194
  50.6 19.7 %collective-permute-done.2 = bf16[84,8,512]{2,1,0:T(8,128)(2,1)} collective-permute-done((bf16[84,8,512]{2,1,0:T(8,128)(2,1)}, bf16[84,8,512]{2,1,0:T(8,128)(2,1)}, u32[]{:S(2)}, u32[]{:S(2)}) %collective-permute-start.2) | collective-permute-done | bytes 688160 | tf_op jit(solution)/shard_map/ppermute | solution.py:204
  70.4 7.1 %collective-permute-done.3 = bf16[84,8,512]{2,1,0:T(8,128)(2,1)} collective-permute-done((bf16[84,8,512]{2,1,0:T(8,128)(2,1)}, bf16[84,8,512]{2,1,0:T(8,128)(2,1)}, u32[]{:S(2)}, u32[]{:S(2)}) %collective-permute-start.3) | collective-permute-done | bytes 688160 | tf_op jit(solution)/shard_map/ppermute | solution.py:204
  77.5 1.1 broadcast_select_fusion
  79.5 1.3 pad.20.ext_ref.refs_3_
  81.8 1.3 pad_slice_fusion.1
  83.1 1.3 pad_slice_fusion.2
  84.4 1.7 fusion.11.zs_ref
  86.1 1.6 fusion.9.zs_ref
  87.7 1.4 copy-done
  89.1 2.9 %copy.25 = bf16[3,512,768]{2,1,0:T(8,128)(2,1)S(1)} copy(bf16[3,512,768]{1,2,0:T(8,128)(2,1)} %bitcast.59) | data formatting | bytes 4718592 | tf_op jit(solution)/shard_map/transpose | solution.py:195
  92.3 1.7 copy-done.1
  93.9 1.6 copy-done.4
  95.6 1.4 copy-done.6
  96.9 3.9 %shard_map.114.refs_2_.refs_3_.refs_4_ = f32[1360,768]{1,0:T(8,128)S(1)} custom-call(bf16[1456,768]{1,0:T(8,128)(2,1)S(1)} %copy-done.4, bf16[1456,512]{1,0:T(8,128)(2,1)S(1)} %copy-done.6, bf16[1360,128]{1,0:T(8,128)(2,1)S(1)} %broadcast_in_dim.2.mask_ref, bf16[2304,512]{1,0:T(8,128)(2,1)S(1)} %bitcast.60, f32[1,512]{1,0:T(1,128)S(1)} %copy-done.8), custom_call_target="tpu_custom_call" | custom-call | flops 3208642560 | bytes 10485760 | tf_op jit(solution)/shard_map/pallas_call | solution.py:256
  100.9 1.0 collective-permute-start.4
  102.5 1.1 copy-done.10
  104.0 1.3 copy-done.2
  106.0 3.9 %shard_map.113.refs_2_.refs_3_ = f32[1360,768]{1,0:T(8,128)S(1)} custom-call(bf16[1456,768]{1,0:T(8,128)(2,1)S(1)} %copy-done.3, bf16[1456,512]{1,0:T(8,128)(2,1)S(1)} %pad.19.ext_ref.refs_4_, bf16[1360,128]{1,0:T(8,128)(2,1)S(1)} %broadcast_in_dim.2.mask_ref, bf16[2304,512]{1,0:T(8,128)(2,1)S(1)} %bitcast.61, f32[1,512]{1,0:T(1,128)S(1)} %copy-done.8), custom_call_target="tpu_custom_call" | custom-call | flops 3208642560 | bytes 10485760 | tf_op jit(solution)/shard_map/pallas_call | solution.py:256
  110.6 3.9 %shard_map.112.refs_2_ = f32[1360,768]{1,0:T(8,128)S(1)} custom-call(bf16[1456,768]{1,0:T(8,128)(2,1)S(1)} %fusion.7.zs_ref, bf16[1456,512]{1,0:T(8,128)(2,1)S(1)} %pad.18.ext_ref.refs_5_, bf16[1360,128]{1,0:T(8,128)(2,1)S(1)} %broadcast_in_dim.2.mask_ref, bf16[2304,512]{1,0:T(8,128)(2,1)S(1)} %bitcast.62, f32[1,512]{1,0:T(1,128)S(1)} %copy-done.8), custom_call_target="tpu_custom_call" | custom-call | flops 3208642560 | bytes 10485760 | tf_op jit(solution)/shard_map/pallas_call | solution.py:256
  114.6 1.3 collective-permute-start.6
  115.9 12.3 %collective-permute-done.6.refs_5_ = bf16[1072,128]{1,0:T(8,128)(2,1)S(1)} collective-permute-done((bf16[1072,128]{1,0:T(8,128)(2,1)S(1)}, bf16[1072,128]{1,0:T(8,128)(2,1)S(1)}, u32[]{:S(2)}, u32[]{:S(2)}) %collective-permute-start.6) | collective-permute-done | bytes 274464 | tf_op jit(solution)/shard_map/ppermute | solution.py:305
  128.2 2.8 %shard_map.118 = (bf16[976,128]{1,0:T(8,128)(2,1)S(1)}, bf16[1536,128]{1,0:T(8,128)(2,1)S(1)}, bf16[1536,512]{1,0:T(8,128)(2,1)S(1)}, f32[976,128]{1,0:T(8,128)S(1)}, f32[976,128]{1,0:T(8,128)S(1)}) custom-call(s32[1]{0:T(128)} %bitcast.15.refs_0_, bf16[1536,768]{1,0:T(8,128)(2,1)S(1)} %bitcast.56, ...), custom_call_target="tpu_custom_call", output_to_operand_aliasing={{1}: (8, {}), {2}: (9, {})} | custom-call | flops 2302672896 | bytes 10485760 | tf_op jit(solution)/shard_map/pallas_call | solution.py:278
  131.0 1.3 collective-permute-start.7
  133.0 1.4 shard_map.123.refs_2_
  134.3 6.0 %collective-permute-done.7.refs_4_ = bf16[976,128]{1,0:T(8,128)(2,1)S(1)} collective-permute-done((bf16[976,128]{1,0:T(8,128)(2,1)S(1)}, bf16[976,128]{1,0:T(8,128)(2,1)S(1)}, u32[]{:S(2)}, u32[]{:S(2)}) %collective-permute-start.7) | collective-permute-done | bytes 249888 | tf_op jit(solution)/shard_map/ppermute | solution.py:305
  140.4 2.6 %shard_map.119 = (bf16[880,128]{1,0:T(8,128)(2,1)S(1)}, bf16[1536,128]{1,0:T(8,128)(2,1)S(1)}, bf16[1536,512]{1,0:T(8,128)(2,1)S(1)}, f32[880,128]{1,0:T(8,128)S(1)}, f32[880,128]{1,0:T(8,128)S(1)}) custom-call(s32[1]{0:T(128)} %bitcast.15.refs_0_, bf16[1536,768]{1,0:T(8,128)(2,1)S(1)} %bitcast.57, ...), custom_call_target="tpu_custom_call", output_to_operand_aliasing={{1}: (7, {}), {2}: (8, {})} | custom-call | flops 2076180480 | bytes 10485760 | tf_op jit(solution)/shard_map/pallas_call | solution.py:278
  143.0 1.3 collective-permute-start.8
  145.6 1.4 shard_map.124.refs_2_
  147.0 4.4 %collective-permute-done.8.refs_3_ = bf16[880,128]{1,0:T(8,128)(2,1)S(1)} collective-permute-done((bf16[880,128]{1,0:T(8,128)(2,1)S(1)}, bf16[880,128]{1,0:T(8,128)(2,1)S(1)}, u32[]{:S(2)}, u32[]{:S(2)}) %collective-permute-start.8) | collective-permute-done | bytes 225312 | tf_op jit(solution)/shard_map/ppermute | solution.py:305
  151.4 3.3 %shard_map.120 = (bf16[784,128]{1,0:T(8,128)(2,1)}, bf16[1536,128]{1,0:T(8,128)(2,1)S(1)}, bf16[1536,512]{1,0:T(8,128)(2,1)S(1)}, f32[784,128]{1,0:T(8,128)}, f32[784,128]{1,0:T(8,128)}) custom-call(s32[1]{0:T(128)} %bitcast.15.refs_0_, bf16[1536,768]{1,0:T(8,128)(2,1)S(1)} %bitcast.58, ...), custom_call_target="tpu_custom_call", output_to_operand_aliasing={{1}: (6, {}), {2}: (7, {})} | custom-call | flops 1849688064 | bytes 10485760 | tf_op jit(solution)/shard_map/pallas_call | solution.py:278
  154.7 1.4 shard_map.125
  156.1 44.2 %all_to_all.20 = bf16[32,72,512]{2,1,0:T(8,128)(2,1)S(1)} all-to-all(bf16[32,72,512]{2,1,0:T(8,128)(2,1)S(1)} %bitcast.63), channel_id=1, replica_groups=mesh['section'=4,'tile'=32] {'tile'}, dimensions={0} | all-to-all | bytes 4718592 | tf_op jit(solution)/shard_map/all_to_all | solution.py:322
  200.6 0.7 copy.37
  201.4 0.8 multiply_subtract_fusion
  (116 shorter events, 7.9 us)
Async XLA Ops:
  1.8 1.6 copy-start.13
  1.8 1.6 copy-start.14
  1.9 1.6 copy-start.15
  4.4 29.5 %collective-permute-start = (bf16[18,32,512]{2,1,0:T(8,128)(2,1)}, bf16[18,32,512]{2,1,0:T(8,128)(2,1)}, u32[]{:S(2)}, u32[]{:S(2)}) collective-permute-start(bf16[18,32,512]{2,1,0:T(8,128)(2,1)} %pad_maximum_fusion.16), channel_id=1, source_target_pairs={{0,8},{1,9},{2,10},{3,11},{4,12},{5,13},{6,14},{7,15},{8,16},{9,17... | collective-permute-start | bytes 1769480 | tf_op jit(solution)/shard_map/ppermute | solution.py:204
  9.4 26.2 %collective-permute-start.1 = (bf16[18,32,512]{2,1,0:T(8,128)(2,1)}, bf16[18,32,512]{2,1,0:T(8,128)(2,1)}, u32[]{:S(2)}, u32[]{:S(2)}) collective-permute-start(bf16[18,32,512]{2,1,0:T(8,128)(2,1)} %pad_maximum_fusion.17), channel_id=1, source_target_pairs={{0,24},{1,25},{2,26},{3,27},{4,28},{5,29},{6,30},{7,31},{8,0},{9,1... | collective-permute-start | bytes 1769480 | tf_op jit(solution)/shard_map/ppermute | solution.py:204
  10.5 26.4 %copy-start.16 = (bf16[16,32,512]{2,1,0:T(8,128)(2,1)}, bf16[16,32,512]{2,1,0:T(8,128)(2,1)S(1)}, u32[]{:S(2)}) copy-start(bf16[16,32,512]{2,1,0:T(8,128)(2,1)S(1)} %get-tuple-element.81) | copy-start | bytes 1572868
  34.0 4.1 %copy-start.22 = (bf16[7,32,512]{2,1,0:T(8,128)(2,1)}, bf16[7,32,512]{2,1,0:T(8,128)(2,1)S(1)}, u32[]{:S(2)}) copy-start(bf16[7,32,512]{2,1,0:T(8,128)(2,1)S(1)} %slice.158) | copy-start | bytes 688132
  34.0 4.0 %copy-start.26 = (bf16[6,32,512]{2,1,0:T(8,128)(2,1)}, bf16[6,32,512]{2,1,0:T(8,128)(2,1)S(1)}, u32[]{:S(2)}) copy-start(bf16[6,32,512]{2,1,0:T(8,128)(2,1)S(1)} %slice.155) | copy-start | bytes 589828
  34.1 4.0 %copy-start.30 = (bf16[5,32,512]{2,1,0:T(8,128)(2,1)}, bf16[5,32,512]{2,1,0:T(8,128)(2,1)S(1)}, u32[]{:S(2)}) copy-start(bf16[5,32,512]{2,1,0:T(8,128)(2,1)S(1)} %slice.152) | copy-start | bytes 491524
  36.7 1.4 copy-start.24
  36.8 1.3 copy-start.28
  36.8 5.5 %copy-start.34 = (f32[1,72,512]{2,1,0:T(8,128)S(1)}, f32[1,72,512]{2,1,0:T(8,128)}, u32[]{:S(2)}) copy-start(f32[1,72,512]{2,1,0:T(8,128)} %param.13) | copy-start | bytes 442372
  36.8 3.0 %copy-start.32 = (bf16[5,32,512]{2,1,0:T(8,128)(2,1)}, bf16[5,32,512]{2,1,0:T(8,128)(2,1)S(1)}, u32[]{:S(2)}) copy-start(bf16[5,32,512]{2,1,0:T(8,128)(2,1)S(1)} %slice.154) | copy-start | bytes 491524
  38.1 32.1 %collective-permute-start.2 = (bf16[84,8,512]{2,1,0:T(8,128)(2,1)}, bf16[84,8,512]{2,1,0:T(8,128)(2,1)}, u32[]{:S(2)}, u32[]{:S(2)}) collective-permute-start(bf16[84,8,512]{2,1,0:T(8,128)(2,1)} %get-tuple-element.77), channel_id=1, source_target_pairs={{0,1},{1,2},{2,3},{3,4},{4,5},{5,6},{6,7},{7,0},{8,9},{9,10},{10,1... | collective-permute-start | bytes 2064392 | tf_op jit(solution)/shard_map/ppermute | solution.py:204
  39.8 37.7 %collective-permute-start.3 = (bf16[84,8,512]{2,1,0:T(8,128)(2,1)}, bf16[84,8,512]{2,1,0:T(8,128)(2,1)}, u32[]{:S(2)}, u32[]{:S(2)}) collective-permute-start(bf16[84,8,512]{2,1,0:T(8,128)(2,1)} %get-tuple-element.78), channel_id=1, source_target_pairs={{0,7},{1,0},{2,1},{3,2},{4,3},{5,4},{6,5},{7,6},{8,15},{9,8},{10,9... | collective-permute-start | bytes 2064392 | tf_op jit(solution)/shard_map/ppermute | solution.py:204
  43.9 43.8 %all-to-all-start = ((bf16[32,72,512]{2,1,0:T(8,128)(2,1)}), bf16[32,72,512]{2,1,0:T(8,128)(2,1)S(1)}, u32[]{:S(2)}, u32[]{:S(2)}) async-start(bf16[32,72,512]{2,1,0:T(8,128)(2,1)} %tile.2), calls=%async_computation | async-start | bytes 4718592 | tf_op jit(solution)/shard_map/all_to_all | solution.py:194
  70.3 8.6 %copy-start.20 = (bf16[84,8,512]{2,1,0:T(8,128)(2,1)}, bf16[84,8,512]{2,1,0:T(8,128)(2,1)S(1)}, u32[]{:S(2)}) copy-start(bf16[84,8,512]{2,1,0:T(8,128)(2,1)S(1)} %broadcast_select_fusion.1) | copy-start | bytes 2064388
  70.3 8.3 %copy-start.17 = (bf16[16,32,512]{2,1,0:T(8,128)(2,1)S(1)}, bf16[16,32,512]{2,1,0:T(8,128)(2,1)}, u32[]{:S(2)}) copy-start(bf16[16,32,512]{2,1,0:T(8,128)(2,1)} %copy-done.16) | copy-start | bytes 1572868
  70.3 8.3 %copy-start.23 = (bf16[7,32,512]{2,1,0:T(8,128)(2,1)S(1)}, bf16[7,32,512]{2,1,0:T(8,128)(2,1)}, u32[]{:S(2)}) copy-start(bf16[7,32,512]{2,1,0:T(8,128)(2,1)} %copy-done.22) | copy-start | bytes 688132
  70.4 8.3 %copy-start.25 = (bf16[7,32,512]{2,1,0:T(8,128)(2,1)S(1)}, bf16[7,32,512]{2,1,0:T(8,128)(2,1)}, u32[]{:S(2)}) copy-start(bf16[7,32,512]{2,1,0:T(8,128)(2,1)} %copy-done.24) | copy-start | bytes 688132
  78.7 2.1 %copy-start.31 = (bf16[5,32,512]{2,1,0:T(8,128)(2,1)S(1)}, bf16[5,32,512]{2,1,0:T(8,128)(2,1)}, u32[]{:S(2)}) copy-start(bf16[5,32,512]{2,1,0:T(8,128)(2,1)} %copy-done.30) | copy-start | bytes 491524
  78.7 2.1 %copy-start.33 = (bf16[5,32,512]{2,1,0:T(8,128)(2,1)S(1)}, bf16[5,32,512]{2,1,0:T(8,128)(2,1)}, u32[]{:S(2)}) copy-start(bf16[5,32,512]{2,1,0:T(8,128)(2,1)} %copy-done.32) | copy-start | bytes 491524
  79.5 1.3 slice-start.1
  79.5 1.3 slice-start.3
  79.5 1.5 slice-start
  79.5 1.6 slice-start.2
  79.5 1.8 copy-start.27
  79.5 1.9 copy-start.29
  81.4 1.7 copy-start.11
  81.5 1.6 copy-start.9
  87.7 1.4 copy-start
  89.1 2.9 %copy-start.37 = (bf16[1360]{0:T(1024)(128)(2,1)S(1)}, bf16[1360]{0:T(1024)(128)(2,1)}, u32[]{:S(2)}) copy-start(bf16[1360]{0:T(1024)(128)(2,1)} %fusion.32) | copy-start | bytes 8164
  89.1 3.1 %copy-start.8 = (f32[1,512]{1,0:T(1,128)S(1)}, f32[1,512]{1,0:T(1,128)}, u32[]{:S(2)}) copy-start(f32[1,512]{1,0:T(1,128)} %bias_ref.5) | copy-start | bytes 6148
  92.3 1.7 copy-start.1
  93.9 1.6 copy-start.4
  95.6 1.4 copy-start.6
  96.9 3.9 %copy-start.7 = (bf16[1456,512]{1,0:T(8,128)(2,1)S(1)}, bf16[1456,512]{1,0:T(8,128)(2,1)}, u32[]{:S(2)}) copy-start(bf16[1456,512]{1,0:T(8,128)(2,1)} %pad.20.ext_ref.refs_3_) | copy-start | bytes 4472836
  100.9 1.3 copy-start.19
  100.9 9.0 %collective-permute-start.4 = (bf16[1264,128]{1,0:T(8,128)(2,1)S(1)}, bf16[1264,128]{1,0:T(8,128)(2,1)S(1)}, u32[]{:S(2)}, u32[]{:S(2)}) collective-permute-start(bf16[1264,128]{1,0:T(8,128)(2,1)S(1)} %get-tuple-element.35), channel_id=1, source_target_pairs={{96,64},{97,65},{98,66},{99,67},{100,68},{101,69},{102,70},{103,71... | collective-permute-start | bytes 970760 | tf_op jit(solution)/shard_map/ppermute | solution.py:305
  102.2 1.3 copy-start.10
  102.2 1.7 copy-start.12
  103.6 1.8 copy-start.2
  103.6 2.4 %copy-start.3 = (bf16[1456,768]{1,0:T(8,128)(2,1)S(1)}, bf16[1456,768]{1,0:T(8,128)(2,1)}, u32[]{:S(2)}) copy-start(bf16[1456,768]{1,0:T(8,128)(2,1)} %fusion.9.zs_ref) | copy-start | bytes 6709252
  109.9 4.6 %collective-permute-start.5 = (bf16[1168,128]{1,0:T(8,128)(2,1)S(1)}, bf16[1168,128]{1,0:T(8,128)(2,1)S(1)}, u32[]{:S(2)}, u32[]{:S(2)}) collective-permute-start(bf16[1168,128]{1,0:T(8,128)(2,1)S(1)} %get-tuple-element.40), channel_id=1, source_target_pairs={{64,32},{96,64},{65,33},{97,65},{66,34},{98,66},{67,35},{99,67},{6... | collective-permute-start | bytes 897032 | tf_op jit(solution)/shard_map/ppermute | solution.py:305
  114.6 13.6 %collective-permute-start.6 = (bf16[1072,128]{1,0:T(8,128)(2,1)S(1)}, bf16[1072,128]{1,0:T(8,128)(2,1)S(1)}, u32[]{:S(2)}, u32[]{:S(2)}) collective-permute-start(bf16[1072,128]{1,0:T(8,128)(2,1)S(1)} %get-tuple-element.45), channel_id=1, source_target_pairs={{32,0},{64,32},{96,64},{33,1},{65,33},{97,65},{34,2},{66,34},{98,6... | collective-permute-start | bytes 823304 | tf_op jit(solution)/shard_map/ppermute | solution.py:305
  128.2 4.1 %copy-start.5 = (bf16[1456,768]{1,0:T(8,128)(2,1)S(1)}, bf16[1456,768]{1,0:T(8,128)(2,1)}, u32[]{:S(2)}) copy-start(bf16[1456,768]{1,0:T(8,128)(2,1)} %fusion.11.zs_ref) | copy-start | bytes 6709252
  131.0 9.4 %collective-permute-start.7 = (bf16[976,128]{1,0:T(8,128)(2,1)S(1)}, bf16[976,128]{1,0:T(8,128)(2,1)S(1)}, u32[]{:S(2)}, u32[]{:S(2)}) collective-permute-start(bf16[976,128]{1,0:T(8,128)(2,1)S(1)} %get-tuple-element.50), channel_id=1, source_target_pairs={{32,0},{64,32},{33,1},{65,33},{34,2},{66,34},{35,3},{67,35},{36,4}... | collective-permute-start | bytes 749576 | tf_op jit(solution)/shard_map/ppermute | solution.py:305
  143.0 8.4 %collective-permute-start.8 = (bf16[880,128]{1,0:T(8,128)(2,1)S(1)}, bf16[880,128]{1,0:T(8,128)(2,1)S(1)}, u32[]{:S(2)}, u32[]{:S(2)}) collective-permute-start(bf16[880,128]{1,0:T(8,128)(2,1)S(1)} %get-tuple-element.55), channel_id=1, source_target_pairs={{32,0},{33,1},{34,2},{35,3},{36,4},{37,5},{38,6},{39,7},{40,8},{41... | collective-permute-start | bytes 675848 | tf_op jit(solution)/shard_map/ppermute | solution.py:305
  (4 other events, 4.1 us)
